TPU v7x, 32 devices: a whole 2x2x4 slice. The times are simulated.
32 devices in a mesh: board: 8 (over y, x, core), hand: 4 (over z).
Axes of the slice: x: 2, y: 2, z: 4, core: 2. Of those that a mesh axis runs over, the one named last changes fastest.
Arguments:
- reach_pre: float32 [1408], P(('board', 'hand')), may hold values from 0.05 to 1
- strategy: bfloat16 [64, 128, 1408], P('board', None, 'hand'), may hold values from 0 to 1
- ranks: int32 [64, 8, 1408], P('board'), may hold values from 0 to 94
- boards: int32 [64, 8, 5], P('board'), may hold values from 0 to 51, as said below
- river_live: int32 [64], P('board'), may hold values from 1 to 8, as said below
- iso_weight: int32 [64], P('board'), may hold values from 1 to 24
- pot: float32 [128], replicated, may hold values from 2 to 24
- line_act: int32 [128], replicated, may hold values from 0 to 2
Outputs:
- preflop_value: float32 [1408], P('hand')
Inputs may be any that keep to these rules, and one draw needn't show every extreme that they name: `boards`: the five cards of a runout are distinct; all runouts of a flop share their first three cards. `river_live`: in every draw some flop has all 8 runouts live.
All inputs are finite; a program needn't handle non-finite values.
Results may differ from a plain program's by a relative error of at most 0.0003.
Values may be sent and summed in bfloat16 or wider, within the bound.
No kernel may reach another device: no remote copies, remote signals or barrier semaphores. Data moves between devices by JAX's collectives and lax.ppermute only.
A program may use at most 64 MiB of HBM per device.

v0:
```python
import jax
import jax.numpy as jnp
import numpy as np
from jax import lax
from jax.sharding import PartitionSpec as P

HANDS = 1326
HPAD = 1408
ACTS = 3


def card_tables():
    first_card, second_card = np.triu_indices(52, 1)
    padding = HPAD - HANDS
    first_card = np.concatenate([first_card, np.full(padding, 52)]).astype(np.int32)
    second_card = np.concatenate([second_card, np.full(padding, 53)]).astype(np.int32)
    alive_mask = np.concatenate([np.ones(HANDS), np.zeros(padding)]).astype(np.float32)
    return (jnp.asarray(first_card), jnp.asarray(second_card), jnp.asarray(alive_mask))


def unblocked(first_rows, second_rows, first_cols, second_cols):
    clear = (first_rows[:, None] != first_cols[None, :]) & (
        first_rows[:, None] != second_cols[None, :]
    )
    clear = (
        clear
        & (second_rows[:, None] != first_cols[None, :])
        & (second_rows[:, None] != second_cols[None, :])
    )
    return clear.astype(jnp.float32)


def live_hands(first_card, second_card, alive_mask, board_cards):
    clear = jnp.all(
        (first_card[:, None] != board_cards[None, :])
        & (second_card[:, None] != board_cards[None, :]),
        axis=1,
    )
    return alive_mask * clear.astype(jnp.float32)


def showdown(rank_rows, rank_cols, live_rows, live_cols, blocking):
    signed = jnp.sign(rank_rows[:, None] - rank_cols[None, :]).astype(jnp.float32)
    return (signed * blocking.astype(jnp.float32) * live_rows[:, None] * live_cols[None, :]).astype(
        jnp.bfloat16
    )


def runout_sum(
    ranks_flop, boards_flop, count_flop, tables, row_span, col_span, blocking, reach_flop
):
    first_card, second_card, alive_mask = tables
    row_start, row_len = row_span
    col_start, col_len = col_span

    def add_runout(runout, acc, factor):
        rank_now = ranks_flop[runout]
        live_now = live_hands(first_card, second_card, alive_mask, boards_flop[runout])
        matrix = showdown(
            lax.dynamic_slice_in_dim(rank_now, row_start, row_len),
            rank_now,
            lax.dynamic_slice_in_dim(live_now, row_start, row_len),
            lax.dynamic_slice_in_dim(live_now, col_start, col_len),
            blocking,
        )
        values = lax.dot_general(
            matrix, reach_flop, (((1,), (1,)), ((), ())), preferred_element_type=jnp.float32
        )
        return acc + values * factor

    empty = jnp.zeros((row_len, reach_flop.shape[0]), jnp.float32)

    def live_step(runout, acc):
        return add_runout(runout, acc, 1.0)

    return lax.fori_loop(0, count_flop, live_step, empty)


def body(reach_pre, strategy, ranks, boards, river_live, iso_weight, pot, line_act):
    tables = card_tables()
    first_card, second_card, alive_mask = tables
    full_reach = lax.all_gather(reach_pre, ("board", "hand"), axis=0, tiled=True)
    local_weight = jnp.sum(iso_weight.astype(jnp.float32))
    weight_total = lax.psum(local_weight, "board")
    total_reach = jnp.sum(full_reach * alive_mask)
    hand_rows = strategy.shape[2]
    slots = full_reach.shape[0]
    row_start = lax.axis_index("hand") * hand_rows
    own_first = lax.dynamic_slice_in_dim(first_card, row_start, hand_rows)
    own_second = lax.dynamic_slice_in_dim(second_card, row_start, hand_rows)
    own_reach = lax.dynamic_slice_in_dim(full_reach, row_start, hand_rows)
    line_reach = (own_reach[None, None, :] * strategy.astype(jnp.float32) / total_reach).astype(
        jnp.bfloat16
    )
    onehot = (line_act[:, None] == jnp.arange(ACTS, dtype=jnp.int32)[None, :]).astype(jnp.float32)
    flop_ids = jnp.arange(strategy.shape[0], dtype=jnp.int32)
    every_reach = lax.all_gather(line_reach, "hand", axis=2, tiled=True)
    blocking = unblocked(own_first, own_second, first_card, second_card).astype(jnp.bfloat16)

    def own_rows(flop_index):
        return runout_sum(
            ranks[flop_index],
            boards[flop_index],
            river_live[flop_index],
            tables,
            (row_start, hand_rows),
            (0, slots),
            blocking,
            every_reach[flop_index],
        )

    acc = lax.map(own_rows, flop_ids)
    line_values = acc * pot[None, None, :] / river_live.astype(jnp.float32)[:, None, None]
    group_values = jnp.dot(
        line_values, onehot, precision=lax.Precision.HIGHEST, preferred_element_type=jnp.float32
    )
    best = jnp.max(group_values, axis=2)
    partial_values = jnp.sum(iso_weight.astype(jnp.float32)[:, None] * best, axis=0)
    summed = lax.psum(partial_values, "board")
    return summed / weight_total


def solution(mesh):
    in_specs = (
        P(("board", "hand")),
        P("board", None, "hand"),
        P("board", None, None),
        P("board", None, None),
        P("board"),
        P("board"),
        P(),
        P(),
    )
    out_specs = P("hand")
    return jax.shard_map(body, mesh=mesh, in_specs=in_specs, out_specs=out_specs, check_vma=False)
```

profile of v0, /device:TPU:0, one launch (start us, length us, event | category | flops | bytes accessed | tf_op | source)
XLA Modules:
  0.0 265.8 jit_solution(16606646617803126494)
XLA Ops:
  6.6 0.9 dynamic-update-slice
  7.5 42.0 %all-reduce = f32[1408]{0:T(1024)S(1)} all-reduce(f32[1408]{0:T(1024)S(1)} %dynamic-update-slice), channel_id=1, replica_groups=mesh['board'=8,'hand'=4] {'board','hand'}, use_global_device_ids=true, to_apply=%add | all-reduce | flops 1408 | bytes 11264
  49.5 1.3 multiply_reduce_fusion.1
  50.8 3.0 %divide_convert_fusion = bf16[8,128,352]{1,0,2:T(8,128)(2,1)} fusion(bf16[8,128,352]{1,2,0:T(8,128)(2,1)} %param.16, f32[]{:T(128)} %multiply_reduce_fusion.1, f32[352]{0:T(512)S(1)} %dynamic_slice.73), kind=kLoop, calls=%fused_computation.17 | loop fusion | flops 1441792 | bytes 1443204 | tf_op jit(solution)/shard_map/convert_element_type | solution.py:92
  54.7 58.5 %all-gather.2.cloned.1.call-done = bf16[8,128,1408]{1,0,2:T(8,128)(2,1)} async-done(((bf16[8,128,352]{1,0,2:T(8,128)(2,1)}), bf16[8,128,1408]{1,0,2:T(8,128)(2,1)}) %all-gather.2.cloned.1.call-update) | async-done | bytes 2883600 | tf_op jit(solution)/shard_map/all_gather | solution.py:97
  113.2 4.8 %copy.19 = bf16[8,128,1408]{2,1,0:T(8,128)(2,1)} copy(bf16[8,128,1408]{1,0,2:T(8,128)(2,1)} %all-gather.2.cloned.1.call-done) | data formatting | bytes 5767168
  118.0 108.5 %while.46 = (s32[]{:T(128)}, f32[8,352,128]{2,1,0:T(8,128)S(1)}, s32[8]{0:T(128)S(1)}, s32[8]{0:T(128)S(1)}, s32[8,8,1408]{2,1,0:T(8,128)}, /*index=5*/s32[8,8,5...) while((s32[]{:T(128)}, f32[8,352,128]{2,1,0:T(8,128)S(1)}, ...), condition=%wide.region_5.6_spmd.clone.clone, body=%wide.region_1.5_spmd.sunk.clone.clone.sunk | while | flops 135376400 | bytes 4126810 | solution.py:112
  120.7 1.0 dynamic-slice_bitcast_fusion.7
  124.7 2.6 while.47
  130.0 1.0 dynamic-slice_bitcast_fusion.7
  134.0 14.0 %while.47 = (s32[]{:T(128)}, f32[352,128]{1,0:T(8,128)S(1)}, s32[]{:T(128)}, s32[8,1408]{1,0:T(8,128)S(1)}, s32[]{:T(128)}, /*index=5*/bf16[352,1408]{1,0:T(8,12...) while((s32[]{:T(128)}, f32[352,128]{1,0:T(8,128)S(1)}, ...), condition=%wide.region_4.4_spmd.clone, body=%wide.region_2.0_spmd.sunk.clone.sunk | while | flops 130915848 | bytes 1768727 | solution.py:76
  135.0 0.9 convolution_add_fusion.2
  140.7 0.9 convolution_add_fusion.2
  142.6 0.9 convolution_add_fusion.2
  150.7 1.0 dynamic-slice_bitcast_fusion.7
  154.7 2.6 while.47
  155.7 0.9 convolution_add_fusion.2
  160.0 1.0 dynamic-slice_bitcast_fusion.7
  163.9 2.6 while.47
  165.0 0.9 convolution_add_fusion.2
  169.2 1.0 dynamic-slice_bitcast_fusion.7
  173.2 8.3 %while.47 = (s32[]{:T(128)}, f32[352,128]{1,0:T(8,128)S(1)}, s32[]{:T(128)}, s32[8,1408]{1,0:T(8,128)S(1)}, s32[]{:T(128)}, /*index=5*/bf16[352,1408]{1,0:T(8,12...) while((s32[]{:T(128)}, f32[352,128]{1,0:T(8,128)S(1)}, ...), condition=%wide.region_4.4_spmd.clone, body=%wide.region_2.0_spmd.sunk.clone.sunk | while | flops 130915848 | bytes 1768727 | solution.py:76
  184.2 1.0 dynamic-slice_bitcast_fusion.7
  188.2 10.2 %while.47 = (s32[]{:T(128)}, f32[352,128]{1,0:T(8,128)S(1)}, s32[]{:T(128)}, s32[8,1408]{1,0:T(8,128)S(1)}, s32[]{:T(128)}, /*index=5*/bf16[352,1408]{1,0:T(8,12...) while((s32[]{:T(128)}, f32[352,128]{1,0:T(8,128)S(1)}, ...), condition=%wide.region_4.4_spmd.clone, body=%wide.region_2.0_spmd.sunk.clone.sunk | while | flops 130915848 | bytes 1768727 | solution.py:76
  196.9 0.9 convolution_add_fusion.2
  201.1 1.0 dynamic-slice_bitcast_fusion.7
  205.1 12.1 %while.47 = (s32[]{:T(128)}, f32[352,128]{1,0:T(8,128)S(1)}, s32[]{:T(128)}, s32[8,1408]{1,0:T(8,128)S(1)}, s32[]{:T(128)}, /*index=5*/bf16[352,1408]{1,0:T(8,12...) while((s32[]{:T(128)}, f32[352,128]{1,0:T(8,128)S(1)}, ...), condition=%wide.region_4.4_spmd.clone, body=%wide.region_2.0_spmd.sunk.clone.sunk | while | flops 130915848 | bytes 1768727 | solution.py:76
  219.9 1.0 dynamic-slice_bitcast_fusion.7
  223.9 2.6 while.47
  226.6 1.1 fusion.6
  227.7 30.0 %all-reduce.1 = (f32[352]{0:T(512)S(1)}, f32[]{:T(128)}) all-reduce(f32[352]{0:T(512)S(1)} %multiply_reduce_fusion, f32[]{:T(128)} %convert_reduce_fusion), channel_id=1, replica_groups=mesh['board'=8,'hand'=4] {'board'}, use_global_device_ids=true, to_apply=%region_8.9 | all-reduce | flops 353 | bytes 2824 | tf_op jit(solution)/shard_map/psum | solution.py:119
  257.8 1.1 broadcast_divide_fusion
  (266 shorter events, 55.5 us)
Async XLA Ops:
  6.5 47.4 %copy-start = (s32[1408]{0:T(1024)S(1)}, s32[1408]{0:T(1024)}, u32[]{:S(2)}) copy-start(s32[1408]{0:T(1024)} %constant.143.clone) | copy-start | bytes 16900
  6.5 47.4 %copy-start.1 = (s32[1408]{0:T(1024)S(1)}, s32[1408]{0:T(1024)}, u32[]{:S(2)}) copy-start(s32[1408]{0:T(1024)} %constant.144.clone) | copy-start | bytes 16900
  6.5 47.5 %copy-start.4 = (s32[8]{0:T(128)S(1)}, s32[8]{0:T(128)}, u32[]{:S(2)}) copy-start(s32[8]{0:T(128)} %param.19) | copy-start | bytes 100
  6.5 47.5 %copy-start.3 = (s32[8]{0:T(128)S(1)}, s32[8]{0:T(128)}, u32[]{:S(2)}) copy-start(s32[8]{0:T(128)} %param.20) | copy-start | bytes 100
  6.5 106.6 %all-gather.2.cloned.1.call-start = ((), (), s32[]{:S(2)}) async-start(), calls=%async_computation | async-start | bytes 3604480 | tf_op jit(solution)/shard_map/all_gather | solution.py:97
  54.7 63.3 %copy-start.2 = (f32[1408]{0:T(1024)S(1)}, f32[1408]{0:T(1024)}, u32[]{:S(2)}) copy-start(f32[1408]{0:T(1024)} %constant.145.clone) | copy-start | bytes 16900
  118.0 108.5 %copy-start.5 = (f32[128]{0:T(128)S(1)}, f32[128]{0:T(128)}, u32[]{:S(2)}) copy-start(f32[128]{0:T(128)} %param.21) | copy-start | bytes 1540
  118.0 108.5 %copy-start.6 = (s32[128]{0:T(128)S(1)}, s32[128]{0:T(128)}, u32[]{:S(2)}) copy-start(s32[128]{0:T(128)} %param.22) | copy-start | bytes 1540
Sparse Core Ops, SparseCore 0:
  54.0 59.1 all-gather.1
where the time goes:
time: 267 us; the launch traced here: 266 us
  blocking collectives  72 us (27%)
  waiting for transfers between devices  58.5 us (22%)
  local copies, waits for them, and re-layouts  43.1 us (16%)
  loops' own time  40.6 us (15%)
  matrix products  23.7 us (9%)
  other arithmetic  14.4 us (5%)
  between operations  13.5 us (5%)
    all_gather x1, waiting for transfers between devices, body(): every_reach = lax.all_gather(line_reach, 'hand', axis=2, tiled=True)  58.5 us
    unnamed x1, blocking collectives  42 us
    psum x1, blocking collectives, body(): summed = lax.psum(partial_values, 'board')  30 us
    another operation x8, loops' own time, runout_sum(): return lax.fori_loop(0, count_flop, live_step, empty)  24.1 us
    dot_general x26, matrix products, add_runout(): lax.dot_general(matrix, reach_flop, (((1,), (1,)), ((), ())), preferred_e...  22.6 us
    another operation x1, loops' own time, body(): acc = lax.map(own_rows, flop_ids)  16.6 us
    squeeze x8, local copies, waits for them, and re-layouts, own_rows(): every_reach[flop_index]  8.15 us
    dynamic_slice x16, local copies, waits for them, and re-layouts, own_rows(): boards[flop_index]  6.53 us
  transfers between devices with their start and end apart: 1, of which 1 were waited for; matrix products, arithmetic and copies ran while one was open for 0% of the time, Pallas kernels for 0%

commit v1 on v0

v1 whole, which is shorter than its diff:
```python
import functools

import jax
import jax.numpy as jnp
import numpy as np
from jax import lax
from jax.experimental import pallas as pl
from jax.experimental.pallas import tpu as pltpu
from jax.sharding import PartitionSpec as P

HANDS = 1326
HPAD = 1408
ACTS = 3
CARDS = 128
DEAD_CARD = 52
GROUP = 4
SPLITS = 3

VMEM = pl.BlockSpec(memory_space=pltpu.VMEM)
SMEM = pl.BlockSpec(memory_space=pltpu.SMEM)
NT = (((1,), (1,)), ((), ()))


def card_incidence():
    first_card, second_card = np.triu_indices(52, 1)
    padding = HPAD - HANDS
    first_card = np.concatenate([first_card, np.full(padding, 52)])
    second_card = np.concatenate([second_card, np.full(padding, 53)])
    table = np.zeros((HPAD, CARDS), np.float32)
    table[np.arange(HPAD), first_card] = 1
    table[np.arange(HPAD), second_card] = 1
    return jnp.asarray(table, jnp.bfloat16)


def params(cost=None, megabytes=48):
    return dict(
        compiler_params=pltpu.CompilerParams(vmem_limit_bytes=megabytes << 20),
        cost_estimate=cost,
    )


def showdown_kernel(
    hand_ref, count_ref, ranks_ref, boards_ref, cards_ref, sums_ref,
    rank_rows, live_rows, columns, spread, clear,
):
    flops, runouts = sums_ref.shape[0], rank_rows.shape[0] // sums_ref.shape[0]
    total = flops * runouts
    rows = sums_ref.shape[1]
    start = pl.multiple_of(hand_ref[0] * rows, 32)
    cards = cards_ref[...]
    own_cards = cards_ref[pl.ds(start, rows), :]

    card_ids = lax.broadcasted_iota(jnp.int32, (total, CARDS), 1)
    on_board = card_ids == DEAD_CARD
    boards = boards_ref[...]
    for place in range(boards.shape[1]):
        on_board = on_board | (card_ids == boards[:, place : place + 1])
    on_board = jnp.where(on_board, 1.0, 0.0).astype(jnp.bfloat16)

    ranks = ranks_ref[...].astype(jnp.float32)
    rank_rows[...] = ranks
    hits = lax.dot_general(on_board, cards, NT, preferred_element_type=jnp.float32)
    live_rows[...] = jnp.maximum(1.0 - hits, 0.0)

    columns[:, :total] = jnp.transpose(ranks, (1, 0))
    columns[:, total:] = jnp.transpose(live_rows[...], (1, 0))
    own_columns = columns[pl.ds(start, rows), :].astype(jnp.bfloat16)

    shared = lax.dot_general(own_cards, cards, NT, preferred_element_type=jnp.float32)
    clear[...] = jnp.maximum(1.0 - shared, 0.0).astype(jnp.bfloat16)

    pick_row = lax.broadcasted_iota(jnp.int32, (2 * total, 256), 0)
    pick_lane = lax.broadcasted_iota(jnp.int32, (2 * total, 256), 1)
    block = 16

    def add_runout(flop, runout, first):
        at = flop * runouts + runout
        pick = pick_row == jnp.where(pick_lane < 128, at, total + at)
        spread[...] = jnp.dot(
            own_columns,
            jnp.where(pick, 1.0, 0.0).astype(jnp.bfloat16),
            preferred_element_type=jnp.float32,
        ).astype(jnp.bfloat16)
        slots = rank_rows.shape[1]
        rank_j = jnp.broadcast_to(rank_rows[pl.ds(at, 1), :], (block, slots)).astype(jnp.bfloat16)
        live_j = jnp.broadcast_to(live_rows[pl.ds(at, 1), :], (block, slots)).astype(jnp.bfloat16)
        for part in range(rows // block):
            span = pl.ds(part * block, block)
            rank_i = spread[span, 0:128]
            live_i = spread[span, 128:256]
            for lane in range(0, slots, 128):
                lanes = pl.ds(lane, 128)
                sign = (rank_i - rank_j[:, lane : lane + 128]) * live_j[:, lane : lane + 128]
                sign = jnp.minimum(jnp.maximum(sign, -live_i), live_i)
                sign = sign * clear[span, lanes]
                if first:
                    sums_ref[flop, span, lanes] = sign
                else:
                    sums_ref[flop, span, lanes] += sign

    def one_flop(flop, carry):
        add_runout(flop, 0, True)

        def more(runout, carry):
            add_runout(flop, runout, False)
            return carry

        return lax.fori_loop(1, count_ref[flop], more, carry)

    lax.fori_loop(0, flops, one_flop, 0)


def showdown_sums(hand, counts, ranks, boards, cards, rows):
    flops, runouts, slots = ranks.shape
    total = flops * runouts
    return pl.pallas_call(
        showdown_kernel,
        out_shape=jax.ShapeDtypeStruct((flops, rows, slots), jnp.bfloat16),
        in_specs=[SMEM, SMEM, VMEM, VMEM, VMEM],
        out_specs=VMEM,
        scratch_shapes=[
            pltpu.VMEM((total, slots), jnp.float32),
            pltpu.VMEM((total, slots), jnp.float32),
            pltpu.VMEM((slots, 2 * total), jnp.float32),
            pltpu.VMEM((rows, 256), jnp.bfloat16),
            pltpu.VMEM((rows, slots), jnp.bfloat16),
        ],
        name="showdown_sums",
        **params(pl.CostEstimate(flops=4 * 10**9, bytes_accessed=10**7, transcendentals=0)),
    )(hand, counts, ranks.reshape(total, slots), boards.reshape(total, -1), cards)


def split_bf16(values):
    parts = []
    for _ in range(SPLITS):
        part = values.astype(jnp.bfloat16).astype(jnp.float32)
        parts.append(part)
        values = values - part
    return parts


def action_kernel(hand_ref, reach_ref, strategy_ref, pot_ref, act_ref, out_ref):
    flops, lines, rows = strategy_ref.shape
    senders, per = reach_ref.shape
    own = rows // per
    reach = reach_ref[...]
    slot = lax.broadcasted_iota(jnp.int32, (senders, per), 0) * per + lax.broadcasted_iota(
        jnp.int32, (senders, per), 1
    )
    alive = jnp.where(slot < HANDS, reach, 0.0)
    total = jnp.sum(jnp.sum(alive, axis=1, keepdims=True), axis=0, keepdims=True)

    mine = reach_ref[pl.ds(pl.multiple_of(hand_ref[0] * own, 8), own), :]
    lane = lax.broadcasted_iota(jnp.int32, (per, rows), 1)
    within = lax.broadcasted_iota(jnp.int32, (per, rows), 0)
    repeat = jnp.where(lax.rem(lane, per) == within, 1.0, 0.0)
    wide = jnp.dot(
        mine, repeat, precision=lax.Precision.HIGHEST, preferred_element_type=jnp.float32
    )
    row_lane = lax.broadcasted_iota(jnp.int32, (own, rows), 1)
    row_id = lax.broadcasted_iota(jnp.int32, (own, rows), 0)
    in_place = (row_lane >= row_id * per) & (row_lane < (row_id + 1) * per)
    own_reach = jnp.sum(jnp.where(in_place, wide, 0.0), axis=0, keepdims=True)
    scale = own_reach / total

    act = act_ref[...]
    row = lax.broadcasted_iota(jnp.int32, (8, lines), 0)
    weights = jnp.where(row == act, jnp.broadcast_to(pot_ref[...], (8, lines)), 0.0)
    weights = jnp.concatenate(split_bf16(weights), axis=0).astype(jnp.bfloat16)
    for flop in range(flops):
        line_reach = (strategy_ref[flop].astype(jnp.float32) * scale).astype(jnp.bfloat16)
        parts = jnp.dot(weights, line_reach, preferred_element_type=jnp.float32)
        sums = parts[0:8] + parts[8:16] + parts[16:24]
        out_ref[flop * GROUP : (flop + 1) * GROUP, :] = sums[0:GROUP]


def action_sums(hand, reach, strategy, pot, line_act):
    flops, lines, rows = strategy.shape
    return pl.pallas_call(
        action_kernel,
        out_shape=jax.ShapeDtypeStruct((flops * GROUP, rows), jnp.float32),
        in_specs=[SMEM, VMEM, VMEM, VMEM, VMEM],
        out_specs=VMEM,
        name="action_sums",
        **params(pl.CostEstimate(flops=10**8, bytes_accessed=10**6, transcendentals=0), 16),
    )(hand, reach, strategy, pot.reshape(1, lines), line_act.reshape(1, lines))


def response_kernel(hand_ref, count_ref, weight_ref, sums_ref, *refs):
    shards, (out_ref,) = refs[:-1], refs[-1:]
    flops, rows, slots = sums_ref.shape
    gathered = jnp.zeros((flops * GROUP, slots), jnp.float32)
    for step, shard in enumerate(shards):
        at = jnp.bitwise_xor(hand_ref[0], step) * rows
        piece = shard[...]
        empty = jnp.zeros((flops * GROUP, slots - rows), jnp.float32)
        gathered = gathered + pltpu.roll(jnp.concatenate([piece, empty], axis=1), at, 1)
    splits = split_bf16(gathered)
    values = jnp.zeros((1, rows), jnp.float32)
    weight_sum = 0
    for pair in range(flops * GROUP // 8):
        left = jnp.concatenate([part[pair * 8 : pair * 8 + 8] for part in splits], axis=0)
        left = left.astype(jnp.bfloat16)
        for flop in range(pair * 8 // GROUP, (pair + 1) * 8 // GROUP):
            parts = lax.dot_general(
                left, sums_ref[flop], NT, preferred_element_type=jnp.float32
            )
            group = parts[0:8] + parts[8:16] + parts[16:24]
            at = flop * GROUP - pair * 8
            best = jnp.max(group[at : at + ACTS], axis=0, keepdims=True)
            weight = weight_ref[flop]
            values = values + best * weight.astype(jnp.float32) / jnp.full(
                (1, rows), count_ref[flop].astype(jnp.float32)
            )
            weight_sum = weight_sum + weight
    tail = jnp.full((1, out_ref.shape[1] - rows), weight_sum.astype(jnp.float32))
    out_ref[...] = jnp.broadcast_to(jnp.concatenate([values, tail], axis=1), out_ref.shape)


def best_response(hand, counts, weights, sums, shards, copies):
    flops, rows, slots = sums.shape
    width = -(-(rows + 1) // 128) * 128
    return pl.pallas_call(
        response_kernel,
        out_shape=jax.ShapeDtypeStruct((copies, width), jnp.float32),
        in_specs=[SMEM, SMEM, SMEM] + [VMEM] * (1 + len(shards)),
        out_specs=VMEM,
        name="best_response",
        **params(pl.CostEstimate(flops=10**9, bytes_accessed=10**7, transcendentals=0)),
    )(hand, counts, weights, sums, *shards)


def body(boards_n, hands_n, reach_pre, strategy, ranks, boards, river_live, iso_weight, pot, line_act):
    everyone = ("board", "hand")
    flops, lines, rows = strategy.shape
    hand = lax.axis_index("hand").astype(jnp.int32).reshape(1)
    devices = boards_n * hands_n

    copies = jnp.broadcast_to(reach_pre[None, :], (devices, reach_pre.shape[0]))
    reach = lax.all_to_all(copies, everyone, 0, 0, tiled=True)
    sums = showdown_sums(hand, river_live, ranks, boards, card_incidence(), rows)

    grouped = action_sums(hand, reach, strategy, pot, line_act)
    shards = [grouped]
    for step in range(1, hands_n):
        swap = [(source, source ^ step) for source in range(hands_n)]
        shards.append(lax.ppermute(grouped, "hand", swap))

    partial = best_response(hand, river_live, iso_weight, sums, shards, boards_n)
    parts = lax.all_to_all(partial, "board", 0, 0, tiled=True)
    whole = jnp.sum(parts, axis=0)
    return whole[:rows] / whole[rows]


def solution(mesh):
    in_specs = (
        P(("board", "hand")),
        P("board", None, "hand"),
        P("board", None, None),
        P("board", None, None),
        P("board"),
        P("board"),
        P(),
        P(),
    )
    run = functools.partial(body, mesh.shape["board"], mesh.shape["hand"])
    return jax.shard_map(run, mesh=mesh, in_specs=in_specs, out_specs=P("hand"), check_vma=False)
```

time: 267 us -> 57.2 us (0.21)
  blocking collectives: 72 us -> 11.1 us
  waiting for transfers between devices: 58.5 us -> 4.84 us
  loops' own time: 40.6 us -> 0 us
  local copies, waits for them, and re-layouts: 43.1 us -> 8.17 us
  matrix products: 23.7 us -> 0 us
  Pallas kernels: 0 us -> 21 us
  between operations: 13.5 us -> 0.07 us
  other arithmetic: 14.4 us -> 1.29 us
  starting transfers between devices: 0.03 us -> 11.7 us
    all_gather x1 -> x0, waiting for transfers between devices: 58.5 us -> none  [body(): every_reach = lax.all_gather(line_reach, 'hand', axis=2, tiled=True)]
    unnamed x1 -> x0, blocking collectives: 42 us -> none
    another operation x9 -> x0, loops' own time: 40.6 us -> none  [the longest x8 24.1 us: runout_sum(): return lax.fori_loop(0, count_flop, live_step, empty)]
    psum x1 -> x0, blocking collectives: 30 us -> none  [body(): summed = lax.psum(partial_values, 'board')]
    dot_general x27 -> x0, matrix products: 23.7 us -> none  [the longest x26 22.6 us: add_runout(): lax.dot_general(matrix, reach_flop, (((1,), (1,)), ((), ())), preferred_e...]
    dynamic_slice x113 -> x0, local copies, waits for them, and re-layouts: 22.3 us -> none  [the longest x16 6.53 us: own_rows(): boards[flop_index]]
    pallas_call x0 -> x3, Pallas kernels: none -> 21 us  [the longest x1 14.8 us: showdown_sums(): pl.pallas_call(showdown_kernel, out_shape=jax.ShapeDtypeStruct((flops, ro...]
    squeeze x16 -> x0, local copies, waits for them, and re-layouts: 14.5 us -> none  [the longest x8 8.15 us: own_rows(): every_reach[flop_index]]
  transfers between devices with their start and end apart: 1 -> 4, of which waited for: 1 -> 1; matrix products, arithmetic and copies ran while one was open for 0% -> 4% of each run, Pallas kernels for 0% -> 25%
where the time goes in v1:
time: 57.2 us; the launch traced here: 58.2 us
  Pallas kernels  21 us (37%)
  starting transfers between devices  11.7 us (20%)
  blocking collectives  11.1 us (19%)
  local copies, waits for them, and re-layouts  8.17 us (14%)
  waiting for transfers between devices  4.84 us (8%)
  other arithmetic  1.29 us (2%)
    pallas_call x1, Pallas kernels, showdown_sums(): pl.pallas_call(showdown_kernel, out_shape=jax.ShapeDtypeStruct((flops, ro...  14.8 us
    all_to_all x1, blocking collectives, body(): parts = lax.all_to_all(partial, 'board', 0, 0, tiled=True)  11.1 us
    all_to_all x1, starting transfers between devices, body(): reach = lax.all_to_all(copies, everyone, 0, 0, tiled=True)  7.3 us
    unnamed x14, local copies, waits for them, and re-layouts  6.25 us
    pallas_call x1, Pallas kernels, best_response(): pl.pallas_call(response_kernel, out_shape=jax.ShapeDtypeStruct((copies, w...  5.71 us
    all_to_all x1, waiting for transfers between devices, body(): reach = lax.all_to_all(copies, everyone, 0, 0, tiled=True)  4.83 us
    ppermute x3, starting transfers between devices, body(): shards.append(lax.ppermute(grouped, 'hand', swap))  4.45 us
    div x1, other arithmetic, body(): return whole[:rows] / whole[rows]  1.26 us
  transfers between devices with their start and end apart: 4, of which 1 were waited for; matrix products, arithmetic and copies ran while one was open for 4% of the time, Pallas kernels for 25%

profile of v1, /device:TPU:0, one launch (start us, length us, event | category | flops | bytes accessed | tf_op | source)
XLA Modules:
  0.0 58.2 jit_solution(3433362233809028636)
XLA Ops:
  0.0 1.3 %broadcast_in_dim.2 = f32[32,1,44]{2,1,0:T(1,128)} broadcast(f32[44]{0:T(128)} %param.9), dimensions={2} | broadcast | bytes 5808 | tf_op jit(solution)/shard_map/broadcast_in_dim | solution.py:239
  1.3 7.3 %all-to-all-start = ((f32[32,1,44]{2,1,0:T(1,128)}), f32[32,1,44]{2,1,0:T(1,128)S(1)}, u32[]{:S(2)}, u32[]{:S(2)}) async-start(f32[32,1,44]{2,1,0:T(1,128)} %broadcast_in_dim.2), calls=%async_computation | async-start | bytes 32768 | tf_op jit(solution)/shard_map/all_to_all | solution.py:240
  8.6 0.8 %copy.12 = s32[8,8,5]{2,1,0:T(8,128)S(1)} copy(s32[8,8,5]{1,0,2:T(8,128)} %param.12) | data formatting | bytes 2560 | tf_op args[3]
  9.4 1.5 %copy.13.strategy_ref = bf16[8,128,352]{2,1,0:T(8,128)(2,1)S(1)} copy(bf16[8,128,352]{1,2,0:T(8,128)(2,1)} %param.10) | data formatting | bytes 1441792 | tf_op args[1]
  10.9 0.0 copy-start.3
  10.9 4.8 %all-to-all-done = f32[32,1,44]{2,1,0:T(1,128)S(1)} async-done(((f32[32,1,44]{2,1,0:T(1,128)}), f32[32,1,44]{2,1,0:T(1,128)S(1)}, u32[]{:S(2)}, u32[]{:S(2)}) %all-to-all-start) | async-done | bytes 5664 | tf_op jit(solution)/shard_map/all_to_all | solution.py:240
  15.7 0.0 copy-start
  15.7 0.7 %copy-done = f32[128]{0:T(128)S(1)} copy-done((f32[128]{0:T(128)S(1)}, f32[128]{0:T(128)}, u32[]{:S(2)}) %copy-start) | copy-done | bytes 536
  16.4 0.0 copy-start.1
  16.4 0.7 %copy-done.1 = s32[128]{0:T(128)S(1)} copy-done((s32[128]{0:T(128)S(1)}, s32[128]{0:T(128)}, u32[]{:S(2)}) %copy-start.1) | copy-done | bytes 536
  17.0 0.4 action_sums.1.refs_0_
  17.5 0.6 %collective-permute-start.2 = (f32[32,352]{1,0:T(8,128)S(1)}, f32[32,352]{1,0:T(8,128)S(1)}, u32[]{:S(2)}, u32[]{:S(2)}) collective-permute-start(f32[32,352]{1,0:T(8,128)S(1)} %action_sums.1.refs_0_), channel_id=1, source_target_pairs={{0,3},{1,2},{2,1},{3,0},{4,7},{5,6},{6,5},{7,4},{8,11},{9,10},{10,... | collective-permute-start | bytes 135176 | tf_op jit(solution)/shard_map/ppermute | solution.py:247
  18.1 1.4 %collective-permute-start.1 = (f32[32,352]{1,0:T(8,128)S(1)}, f32[32,352]{1,0:T(8,128)S(1)}, u32[]{:S(2)}, u32[]{:S(2)}) collective-permute-start(f32[32,352]{1,0:T(8,128)S(1)} %action_sums.1.refs_0_), channel_id=1, source_target_pairs={{0,2},{1,3},{2,0},{3,1},{4,6},{5,7},{6,4},{7,5},{8,10},{9,11},{10,... | collective-permute-start | bytes 135176 | tf_op jit(solution)/shard_map/ppermute | solution.py:247
  19.5 2.4 %collective-permute-start = (f32[32,352]{1,0:T(8,128)S(1)}, f32[32,352]{1,0:T(8,128)S(1)}, u32[]{:S(2)}, u32[]{:S(2)}) collective-permute-start(f32[32,352]{1,0:T(8,128)S(1)} %action_sums.1.refs_0_), channel_id=1, source_target_pairs={{0,1},{1,0},{2,3},{3,2},{4,5},{5,4},{6,7},{7,6},{8,9},{9,8},{10,11... | collective-permute-start | bytes 135176 | tf_op jit(solution)/shard_map/ppermute | solution.py:247
  21.9 0.0 copy-start.2
  21.9 0.7 %copy-done.2 = s32[8]{0:T(128)S(1)} copy-done((s32[8]{0:T(128)S(1)}, s32[8]{0:T(128)}, u32[]{:S(2)}) %copy-start.2) | copy-done | bytes 56
  22.6 0.0 copy-start.4
  22.6 1.0 %copy-done.4 = s32[8,8,1408]{2,1,0:T(8,128)S(1)} copy-done((s32[8,8,1408]{2,1,0:T(8,128)S(1)}, s32[8,8,1408]{2,1,0:T(8,128)}, u32[]{:S(2)}) %copy-start.4) | copy-done | bytes 360472
  23.6 0.0 copy-start.5
  23.6 1.0 %copy-done.5 = bf16[1408,128]{1,0:T(8,128)(2,1)S(1)} copy-done((bf16[1408,128]{1,0:T(8,128)(2,1)S(1)}, bf16[1408,128]{1,0:T(8,128)(2,1)}, u32[]{:S(2)}) %copy-start.5) | copy-done | bytes 360472
  24.6 14.8 %showdown_sums.1.sums_ref = bf16[8,352,1408]{2,1,0:T(8,128)(2,1)} custom-call(s32[1]{0:T(128)} %bitcast.hand_ref, s32[8]{0:T(128)S(1)} %copy-done.2, s32[64,1408]{1,0:T(8,128)S(1)} %bitcast.13, s32[64,5]{1,0:T(8,128)S(1)} %bitcast.10, bf16[1408,128]{1,0:T(8,128)(2,1)S(1)} %copy-done.5), custom_call_target="tpu_custom_call" | custom-call | flops 4000000000 | bytes 10000000 | tf_op jit(solution)/shard_map/showdown_sums/pallas_call | solution.py:116
  39.4 0.0 collective-permute-done.2.refs_3_
  39.4 0.0 collective-permute-done.1.refs_2_
  39.4 0.0 collective-permute-done.refs_1_
  39.4 0.0 copy-done.3
  39.4 5.7 %best_response.1 = f32[8,384]{1,0:T(8,128)S(1)} custom-call(s32[1]{0:T(128)} %bitcast.hand_ref, s32[8]{0:T(128)S(1)} %copy-done.2, s32[8]{0:T(128)S(1)} %copy-done.3, bf16[8,352,1408]{2,1,0:T(8,128)(2,1)} %showdown_sums.1.sums_ref, f32[32,352]{1,0:T(8,128)S(1)} %action_sums.1.refs_0_, f32[32,352]{1,0:T(8,128)S(1)} %collective-permute-done.refs_1_, ...), custom_call_target="tpu_custom_call" | custom-call | flops 1000000000 | bytes 10000000 | tf_op jit(solution)/shard_map/best_response/pallas_call | solution.py:223
  45.2 11.1 %all_to_all.17 = f32[8,1,384]{2,1,0:T(1,128)S(1)} all-to-all(f32[8,1,384]{2,1,0:T(1,128)S(1)} %copy.14), channel_id=1, replica_groups=mesh['board'=8,'hand'=4] {'board'}, dimensions={0} | all-to-all | bytes 24576 | tf_op jit(solution)/shard_map/all_to_all | solution.py:250
  56.3 0.7 %slice.7 = f32[1]{0:T(128)} slice(f32[384]{0:T(512)S(1)} %reduce_sum.9), slice={[352:353]} | slice | bytes 8 | tf_op jit(solution)/shard_map/slice | solution.py:252
  56.9 1.3 %slice_divide_fusion = f32[352]{0:T(512)} fusion(f32[384]{0:T(512)S(1)} %reduce_sum.9, f32[]{:T(128)} %bitcast.7), kind=kLoop, calls=%fused_computation | loop fusion | flops 352 | bytes 2820 | tf_op jit(solution)/shard_map/div | solution.py:252
  (2 shorter events, 0.0 us)
Async XLA Ops:
  1.3 14.5 %all-to-all-start = ((f32[32,1,44]{2,1,0:T(1,128)}), f32[32,1,44]{2,1,0:T(1,128)S(1)}, u32[]{:S(2)}, u32[]{:S(2)}) async-start(f32[32,1,44]{2,1,0:T(1,128)} %broadcast_in_dim.2), calls=%async_computation | async-start | bytes 32768 | tf_op jit(solution)/shard_map/all_to_all | solution.py:240
  10.9 28.5 %copy-start.3 = (s32[8]{0:T(128)S(1)}, s32[8]{0:T(128)}, u32[]{:S(2)}) copy-start(s32[8]{0:T(128)} %weight_ref.1) | copy-start | bytes 100
  15.7 0.7 %copy-start = (f32[128]{0:T(128)S(1)}, f32[128]{0:T(128)}, u32[]{:S(2)}) copy-start(f32[128]{0:T(128)} %param.15) | copy-start | bytes 1540
  16.4 0.7 %copy-start.1 = (s32[128]{0:T(128)S(1)}, s32[128]{0:T(128)}, u32[]{:S(2)}) copy-start(s32[128]{0:T(128)} %param.16) | copy-start | bytes 1540
  17.5 21.9 %collective-permute-start.2 = (f32[32,352]{1,0:T(8,128)S(1)}, f32[32,352]{1,0:T(8,128)S(1)}, u32[]{:S(2)}, u32[]{:S(2)}) collective-permute-start(f32[32,352]{1,0:T(8,128)S(1)} %action_sums.1.refs_0_), channel_id=1, source_target_pairs={{0,3},{1,2},{2,1},{3,0},{4,7},{5,6},{6,5},{7,4},{8,11},{9,10},{10,... | collective-permute-start | bytes 135176 | tf_op jit(solution)/shard_map/ppermute | solution.py:247
  18.1 21.3 %collective-permute-start.1 = (f32[32,352]{1,0:T(8,128)S(1)}, f32[32,352]{1,0:T(8,128)S(1)}, u32[]{:S(2)}, u32[]{:S(2)}) collective-permute-start(f32[32,352]{1,0:T(8,128)S(1)} %action_sums.1.refs_0_), channel_id=1, source_target_pairs={{0,2},{1,3},{2,0},{3,1},{4,6},{5,7},{6,4},{7,5},{8,10},{9,11},{10,... | collective-permute-start | bytes 135176 | tf_op jit(solution)/shard_map/ppermute | solution.py:247
  19.5 19.9 %collective-permute-start = (f32[32,352]{1,0:T(8,128)S(1)}, f32[32,352]{1,0:T(8,128)S(1)}, u32[]{:S(2)}, u32[]{:S(2)}) collective-permute-start(f32[32,352]{1,0:T(8,128)S(1)} %action_sums.1.refs_0_), channel_id=1, source_target_pairs={{0,1},{1,0},{2,3},{3,2},{4,5},{5,4},{6,7},{7,6},{8,9},{9,8},{10,11... | collective-permute-start | bytes 135176 | tf_op jit(solution)/shard_map/ppermute | solution.py:247
  21.9 0.7 %copy-start.2 = (s32[8]{0:T(128)S(1)}, s32[8]{0:T(128)}, u32[]{:S(2)}) copy-start(s32[8]{0:T(128)} %count_ref.3) | copy-start | bytes 100
  22.6 1.0 %copy-start.4 = (s32[8,8,1408]{2,1,0:T(8,128)S(1)}, s32[8,8,1408]{2,1,0:T(8,128)}, u32[]{:S(2)}) copy-start(s32[8,8,1408]{2,1,0:T(8,128)} %param.11) | copy-start | bytes 1081348
  23.6 1.0 %copy-start.5 = (bf16[1408,128]{1,0:T(8,128)(2,1)S(1)}, bf16[1408,128]{1,0:T(8,128)(2,1)}, u32[]{:S(2)}) copy-start(bf16[1408,128]{1,0:T(8,128)(2,1)} %constant.8.clone.cards_ref) | copy-start | bytes 1081348
